TPU v7x, 32 devices: a whole 2x2x4 slice. The times are simulated.
32 devices in a mesh: rows: 8 (over y, x, core), rep: 4 (over z).
Axes of the slice: x: 2, y: 2, z: 4, core: 2. Of those that a mesh axis runs over, the one named last changes fastest.
Arguments:
- weights: bfloat16 [80, 524288], P('rep', 'rows'), may hold values from 0.25 to 4
- cell_ids: int32 [524288], P('rows'), may hold values from 0 to 31
- group_sizes: int32 [8, 1024], P('rows'), may hold values from 32 to 96, as said below
- group_county: int32 [8192, 1], P('rows'), may hold values from 0 to 255; in each aligned block of 1024 rows (0 to 1023, 1024 to 2047, ...) at most 10 rows name the same one
- age_rate: float32 [256, 4], P('rows'), may hold values from 8 to 40
- kind_rate: float32 [256, 8], P('rows'), may hold values from 2 to 20
Outputs:
- raked: float32 [8192, 2560], P('rows', 'rep')
- spread: float32 [8192, 32], P('rows')
Inputs may be any that keep to these rules, and one draw needn't show every extreme that they name: `group_sizes`: each shard's 1024 sizes sum to 65536. `group_county`: among the 1024 block groups of one shard, no county holds more than 10.
All inputs are finite; a program needn't handle non-finite values.
Results may differ from a plain program's by a relative error of at most 0.0003.
Values sent between devices are 32-bit elements; how exact they have to be, the bound alone decides.
A program may use at most 64 MiB of HBM per device.

v0:
```python
import jax
import jax.numpy as jnp
from jax import lax
from jax.sharding import PartitionSpec as P

AGES = 4
KINDS = 8
CELLS = 32
LOW = 32
ITERS = 4


def rake(county_tables, groups_in, age_rate, kind_rate):
    county_rows = county_tables.shape[0]
    current = county_tables.reshape(county_rows, -1, AGES, KINDS)
    age_goal = (age_rate * groups_in[:, None])[:, None, :]
    kind_goal = (kind_rate * groups_in[:, None])[:, None, :]
    factor = jnp.ones_like(current)
    for sweep_index in range(ITERS):
        ratios = age_goal / jnp.maximum(jnp.sum(current, axis=3), 1.0)
        current = current * ratios[:, :, :, None]
        factor = factor * ratios[:, :, :, None]
        ratios = kind_goal / jnp.maximum(jnp.sum(current, axis=2), 1.0)
        current = current * ratios[:, :, None, :]
        factor = factor * ratios[:, :, None, :]
    return factor.reshape(county_rows, -1)


def exact_dot(left, right):
    return jnp.dot(left, right, precision=lax.Precision.HIGHEST, preferred_element_type=jnp.float32)


def tabulate(weights, cell_ids, group_sizes):
    reps_here, records_here = weights.shape
    group_here = group_sizes.shape[1]
    row_width = reps_here * CELLS
    block_rows = min(4096, records_here)
    window = block_rows // LOW + 2
    group_range = jnp.arange(group_here, dtype=jnp.int32)
    upper = (group_range[:, None] <= group_range[None, :]).astype(jnp.float32)
    sizes_float = group_sizes.astype(jnp.float32)
    group_ends = exact_dot(sizes_float, upper)[0].astype(jnp.int32)
    group_starts = group_ends - group_sizes[0]
    beyond = jnp.full((window,), records_here + 1, jnp.int32)
    ends_padded = jnp.concatenate([group_ends, beyond])
    starts_padded = jnp.concatenate([group_starts, beyond])
    cell_range = jnp.arange(CELLS, dtype=jnp.int32)
    block_range = jnp.arange(block_rows, dtype=jnp.int32)

    def add_block(block_index, totals):
        start = block_index * block_rows
        weight_block = lax.dynamic_slice_in_dim(weights, start, block_rows, 1)
        cell_block = lax.dynamic_slice_in_dim(cell_ids, start, block_rows, 0)
        first_slot = jnp.sum((group_ends <= start).astype(jnp.int32))
        ends_window = lax.dynamic_slice_in_dim(ends_padded, first_slot, window, 0)
        starts_window = lax.dynamic_slice_in_dim(starts_padded, first_slot, window, 0)
        place = start + block_range
        slot_hot = (
            (place[:, None] >= starts_window[None, :]) & (place[:, None] < ends_window[None, :])
        ).astype(jnp.bfloat16)
        cell_hot = (cell_block[None, None, :] == cell_range[None, :, None]).astype(jnp.bfloat16)
        spread_cells = (weight_block[:, None, :] * cell_hot).reshape(row_width, block_rows)
        product = jnp.dot(spread_cells, slot_hot, preferred_element_type=jnp.float32)
        current = lax.dynamic_slice_in_dim(totals, first_slot, window, 1)
        return lax.dynamic_update_slice_in_dim(totals, current + product, first_slot, 1)

    totals = jnp.zeros((row_width, group_here + window), jnp.float32)
    totals = lax.fori_loop(0, records_here // block_rows, add_block, totals)
    return totals[:, :group_here].T


def county_partials(tables, county_hot):
    partial_value = exact_dot(county_hot.T, tables)
    member = jnp.sum(county_hot, axis=0)
    return (partial_value, member)


def local(weights, cell_ids, group_sizes, group_county, age_rate, kind_rate):
    tables = tabulate(weights, cell_ids, group_sizes)
    group_here, row_width = tables.shape
    county_ids = group_county[:, 0]
    owners = lax.axis_size("rows")
    county_here = age_rate.shape[0]
    counties = county_here * owners
    county_range = jnp.arange(counties, dtype=jnp.int32)
    county_hot = (county_ids[:, None] == county_range[None, :]).astype(jnp.float32)
    partial_value, member = county_partials(tables, county_hot)
    county_tables, groups_in = (
        lax.psum_scatter(partial_value, "rows", scatter_dimension=0, tiled=True),
        lax.psum_scatter(member, "rows", scatter_dimension=0, tiled=True),
    )
    factor = rake(county_tables, groups_in, age_rate, kind_rate)
    all_factors = lax.all_gather(factor, "rows", axis=0, tiled=True)
    raked = tables * exact_dot(county_hot, all_factors)
    reps_here = row_width // CELLS
    shaped = raked.reshape(group_here, reps_here, CELLS)
    total_reps = reps_here * lax.axis_size("rep")
    centre = lax.psum(jnp.sum(shaped, axis=1), "rep") / total_reps
    deviation = lax.psum(jnp.sum(jnp.square(shaped - centre[:, None, :]), axis=1), "rep")
    return (raked, deviation * (4.0 / total_reps))


def solution(mesh):
    placed = (
        P("rep", "rows"),
        P("rows"),
        P("rows", None),
        P("rows", None),
        P("rows", None),
        P("rows", None),
    )
    return jax.shard_map(
        local,
        mesh=mesh,
        in_specs=placed,
        out_specs=(P("rows", "rep"), P("rows", None)),
        check_vma=False,
    )
```

profile of v0, /device:TPU:0, one launch (start us, length us, event | category | flops | bytes accessed | tf_op | source)
XLA Modules:
  0.0 367.9 jit_solution(5523735008572708595)
XLA Ops:
  9.5 216.6 %while.14 = (s32[]{:T(128)}, f32[640,1154]{0,1:T(8,128)S(1)}, s32[1024]{0:T(1024)S(1)}, bf16[20,65536]{1,0:T(8,128)(2,1)}, s32[65536]{0:T(1024)}, /*index=5*/s32...) while((s32[]{:T(128)}, f32[640,1154]{0,1:T(8,128)S(1)}, ...), condition=%wide.region_2.0_spmd.clone, body=%wide.region_0.0_spmd.clone.sunk | while | flops 686145792 | bytes 12922137 | solution.py:68
  11.2 2.8 broadcast_multiply_fusion.6
  16.7 4.3 %fusion.35 = f32[640,130]{0,1:T(8,128)S(1)} fusion(bf16[640,4096]{1,0:T(8,128)(2,1)} %bitcast.20, s32[4096]{0:T(1024)S(1)} %iota_add_fusion.2, s32[130]{0:T(256)S(1)} %dynamic_slice.50, s32[130]{0:T(256)S(1)} %dynamic_slice.51, f32[640,1154]{0,1:T(8,128)S(1)} %get-tuple-element.252, s32[]{:T(128)S(6)} %select_n.23), kind=kOutput, calls=%fused_computation.7.clone.1 | convolution fusion | flops 683255040 | bytes 5925908 | tf_op jit(solution)/shard_map/while/body/eval_jaxpr/dot_general | solution.py:63
  24.7 2.8 broadcast_multiply_fusion.6
  30.2 4.3 %fusion.35 = f32[640,130]{0,1:T(8,128)S(1)} fusion(bf16[640,4096]{1,0:T(8,128)(2,1)} %bitcast.20, s32[4096]{0:T(1024)S(1)} %iota_add_fusion.2, s32[130]{0:T(256)S(1)} %dynamic_slice.50, s32[130]{0:T(256)S(1)} %dynamic_slice.51, f32[640,1154]{0,1:T(8,128)S(1)} %get-tuple-element.252, s32[]{:T(128)S(6)} %select_n.23), kind=kOutput, calls=%fused_computation.7.clone.1 | convolution fusion | flops 683255040 | bytes 5925908 | tf_op jit(solution)/shard_map/while/body/eval_jaxpr/dot_general | solution.py:63
  34.6 1.9 dynamic_update_slice.9
  38.3 2.8 broadcast_multiply_fusion.6
  43.8 4.3 %fusion.35 = f32[640,130]{0,1:T(8,128)S(1)} fusion(bf16[640,4096]{1,0:T(8,128)(2,1)} %bitcast.20, s32[4096]{0:T(1024)S(1)} %iota_add_fusion.2, s32[130]{0:T(256)S(1)} %dynamic_slice.50, s32[130]{0:T(256)S(1)} %dynamic_slice.51, f32[640,1154]{0,1:T(8,128)S(1)} %get-tuple-element.252, s32[]{:T(128)S(6)} %select_n.23), kind=kOutput, calls=%fused_computation.7.clone.1 | convolution fusion | flops 683255040 | bytes 5925908 | tf_op jit(solution)/shard_map/while/body/eval_jaxpr/dot_general | solution.py:63
  48.1 1.9 dynamic_update_slice.9
  51.8 2.8 broadcast_multiply_fusion.6
  57.3 4.3 %fusion.35 = f32[640,130]{0,1:T(8,128)S(1)} fusion(bf16[640,4096]{1,0:T(8,128)(2,1)} %bitcast.20, s32[4096]{0:T(1024)S(1)} %iota_add_fusion.2, s32[130]{0:T(256)S(1)} %dynamic_slice.50, s32[130]{0:T(256)S(1)} %dynamic_slice.51, f32[640,1154]{0,1:T(8,128)S(1)} %get-tuple-element.252, s32[]{:T(128)S(6)} %select_n.23), kind=kOutput, calls=%fused_computation.7.clone.1 | convolution fusion | flops 683255040 | bytes 5925908 | tf_op jit(solution)/shard_map/while/body/eval_jaxpr/dot_general | solution.py:63
  61.7 1.9 dynamic_update_slice.9
  65.4 2.8 broadcast_multiply_fusion.6
  70.9 4.3 %fusion.35 = f32[640,130]{0,1:T(8,128)S(1)} fusion(bf16[640,4096]{1,0:T(8,128)(2,1)} %bitcast.20, s32[4096]{0:T(1024)S(1)} %iota_add_fusion.2, s32[130]{0:T(256)S(1)} %dynamic_slice.50, s32[130]{0:T(256)S(1)} %dynamic_slice.51, f32[640,1154]{0,1:T(8,128)S(1)} %get-tuple-element.252, s32[]{:T(128)S(6)} %select_n.23), kind=kOutput, calls=%fused_computation.7.clone.1 | convolution fusion | flops 683255040 | bytes 5925908 | tf_op jit(solution)/shard_map/while/body/eval_jaxpr/dot_general | solution.py:63
  75.2 1.9 dynamic_update_slice.9
  78.9 2.8 broadcast_multiply_fusion.6
  84.4 4.3 %fusion.35 = f32[640,130]{0,1:T(8,128)S(1)} fusion(bf16[640,4096]{1,0:T(8,128)(2,1)} %bitcast.20, s32[4096]{0:T(1024)S(1)} %iota_add_fusion.2, s32[130]{0:T(256)S(1)} %dynamic_slice.50, s32[130]{0:T(256)S(1)} %dynamic_slice.51, f32[640,1154]{0,1:T(8,128)S(1)} %get-tuple-element.252, s32[]{:T(128)S(6)} %select_n.23), kind=kOutput, calls=%fused_computation.7.clone.1 | convolution fusion | flops 683255040 | bytes 5925908 | tf_op jit(solution)/shard_map/while/body/eval_jaxpr/dot_general | solution.py:63
  88.8 1.9 dynamic_update_slice.9
  92.5 2.8 broadcast_multiply_fusion.6
  98.0 4.3 %fusion.35 = f32[640,130]{0,1:T(8,128)S(1)} fusion(bf16[640,4096]{1,0:T(8,128)(2,1)} %bitcast.20, s32[4096]{0:T(1024)S(1)} %iota_add_fusion.2, s32[130]{0:T(256)S(1)} %dynamic_slice.50, s32[130]{0:T(256)S(1)} %dynamic_slice.51, f32[640,1154]{0,1:T(8,128)S(1)} %get-tuple-element.252, s32[]{:T(128)S(6)} %select_n.23), kind=kOutput, calls=%fused_computation.7.clone.1 | convolution fusion | flops 683255040 | bytes 5925908 | tf_op jit(solution)/shard_map/while/body/eval_jaxpr/dot_general | solution.py:63
  106.0 2.8 broadcast_multiply_fusion.6
  111.5 4.3 %fusion.35 = f32[640,130]{0,1:T(8,128)S(1)} fusion(bf16[640,4096]{1,0:T(8,128)(2,1)} %bitcast.20, s32[4096]{0:T(1024)S(1)} %iota_add_fusion.2, s32[130]{0:T(256)S(1)} %dynamic_slice.50, s32[130]{0:T(256)S(1)} %dynamic_slice.51, f32[640,1154]{0,1:T(8,128)S(1)} %get-tuple-element.252, s32[]{:T(128)S(6)} %select_n.23), kind=kOutput, calls=%fused_computation.7.clone.1 | convolution fusion | flops 683255040 | bytes 5925908 | tf_op jit(solution)/shard_map/while/body/eval_jaxpr/dot_general | solution.py:63
  119.5 2.8 broadcast_multiply_fusion.6
  125.1 4.3 %fusion.35 = f32[640,130]{0,1:T(8,128)S(1)} fusion(bf16[640,4096]{1,0:T(8,128)(2,1)} %bitcast.20, s32[4096]{0:T(1024)S(1)} %iota_add_fusion.2, s32[130]{0:T(256)S(1)} %dynamic_slice.50, s32[130]{0:T(256)S(1)} %dynamic_slice.51, f32[640,1154]{0,1:T(8,128)S(1)} %get-tuple-element.252, s32[]{:T(128)S(6)} %select_n.23), kind=kOutput, calls=%fused_computation.7.clone.1 | convolution fusion | flops 683255040 | bytes 5925908 | tf_op jit(solution)/shard_map/while/body/eval_jaxpr/dot_general | solution.py:63
  133.1 2.8 broadcast_multiply_fusion.6
  138.6 4.3 %fusion.35 = f32[640,130]{0,1:T(8,128)S(1)} fusion(bf16[640,4096]{1,0:T(8,128)(2,1)} %bitcast.20, s32[4096]{0:T(1024)S(1)} %iota_add_fusion.2, s32[130]{0:T(256)S(1)} %dynamic_slice.50, s32[130]{0:T(256)S(1)} %dynamic_slice.51, f32[640,1154]{0,1:T(8,128)S(1)} %get-tuple-element.252, s32[]{:T(128)S(6)} %select_n.23), kind=kOutput, calls=%fused_computation.7.clone.1 | convolution fusion | flops 683255040 | bytes 5925908 | tf_op jit(solution)/shard_map/while/body/eval_jaxpr/dot_general | solution.py:63
  146.6 2.8 broadcast_multiply_fusion.6
  152.2 4.3 %fusion.35 = f32[640,130]{0,1:T(8,128)S(1)} fusion(bf16[640,4096]{1,0:T(8,128)(2,1)} %bitcast.20, s32[4096]{0:T(1024)S(1)} %iota_add_fusion.2, s32[130]{0:T(256)S(1)} %dynamic_slice.50, s32[130]{0:T(256)S(1)} %dynamic_slice.51, f32[640,1154]{0,1:T(8,128)S(1)} %get-tuple-element.252, s32[]{:T(128)S(6)} %select_n.23), kind=kOutput, calls=%fused_computation.7.clone.1 | convolution fusion | flops 683255040 | bytes 5925908 | tf_op jit(solution)/shard_map/while/body/eval_jaxpr/dot_general | solution.py:63
  160.2 2.8 broadcast_multiply_fusion.6
  165.7 4.3 %fusion.35 = f32[640,130]{0,1:T(8,128)S(1)} fusion(bf16[640,4096]{1,0:T(8,128)(2,1)} %bitcast.20, s32[4096]{0:T(1024)S(1)} %iota_add_fusion.2, s32[130]{0:T(256)S(1)} %dynamic_slice.50, s32[130]{0:T(256)S(1)} %dynamic_slice.51, f32[640,1154]{0,1:T(8,128)S(1)} %get-tuple-element.252, s32[]{:T(128)S(6)} %select_n.23), kind=kOutput, calls=%fused_computation.7.clone.1 | convolution fusion | flops 683255040 | bytes 5925908 | tf_op jit(solution)/shard_map/while/body/eval_jaxpr/dot_general | solution.py:63
  170.0 1.9 dynamic_update_slice.9
  173.7 2.8 broadcast_multiply_fusion.6
  179.2 4.3 %fusion.35 = f32[640,130]{0,1:T(8,128)S(1)} fusion(bf16[640,4096]{1,0:T(8,128)(2,1)} %bitcast.20, s32[4096]{0:T(1024)S(1)} %iota_add_fusion.2, s32[130]{0:T(256)S(1)} %dynamic_slice.50, s32[130]{0:T(256)S(1)} %dynamic_slice.51, f32[640,1154]{0,1:T(8,128)S(1)} %get-tuple-element.252, s32[]{:T(128)S(6)} %select_n.23), kind=kOutput, calls=%fused_computation.7.clone.1 | convolution fusion | flops 683255040 | bytes 5925908 | tf_op jit(solution)/shard_map/while/body/eval_jaxpr/dot_general | solution.py:63
  187.3 2.8 broadcast_multiply_fusion.6
  192.8 4.3 %fusion.35 = f32[640,130]{0,1:T(8,128)S(1)} fusion(bf16[640,4096]{1,0:T(8,128)(2,1)} %bitcast.20, s32[4096]{0:T(1024)S(1)} %iota_add_fusion.2, s32[130]{0:T(256)S(1)} %dynamic_slice.50, s32[130]{0:T(256)S(1)} %dynamic_slice.51, f32[640,1154]{0,1:T(8,128)S(1)} %get-tuple-element.252, s32[]{:T(128)S(6)} %select_n.23), kind=kOutput, calls=%fused_computation.7.clone.1 | convolution fusion | flops 683255040 | bytes 5925908 | tf_op jit(solution)/shard_map/while/body/eval_jaxpr/dot_general | solution.py:63
  200.8 2.8 broadcast_multiply_fusion.6
  206.3 4.3 %fusion.35 = f32[640,130]{0,1:T(8,128)S(1)} fusion(bf16[640,4096]{1,0:T(8,128)(2,1)} %bitcast.20, s32[4096]{0:T(1024)S(1)} %iota_add_fusion.2, s32[130]{0:T(256)S(1)} %dynamic_slice.50, s32[130]{0:T(256)S(1)} %dynamic_slice.51, f32[640,1154]{0,1:T(8,128)S(1)} %get-tuple-element.252, s32[]{:T(128)S(6)} %select_n.23), kind=kOutput, calls=%fused_computation.7.clone.1 | convolution fusion | flops 683255040 | bytes 5925908 | tf_op jit(solution)/shard_map/while/body/eval_jaxpr/dot_general | solution.py:63
  214.3 2.8 broadcast_multiply_fusion.6
  219.8 4.3 %fusion.35 = f32[640,130]{0,1:T(8,128)S(1)} fusion(bf16[640,4096]{1,0:T(8,128)(2,1)} %bitcast.20, s32[4096]{0:T(1024)S(1)} %iota_add_fusion.2, s32[130]{0:T(256)S(1)} %dynamic_slice.50, s32[130]{0:T(256)S(1)} %dynamic_slice.51, f32[640,1154]{0,1:T(8,128)S(1)} %get-tuple-element.252, s32[]{:T(128)S(6)} %select_n.23), kind=kOutput, calls=%fused_computation.7.clone.1 | convolution fusion | flops 683255040 | bytes 5925908 | tf_op jit(solution)/shard_map/while/body/eval_jaxpr/dot_general | solution.py:63
  227.7 3.3 copy.19
  231.1 2.7 fusion.16
  235.4 15.2 %all-reduce.2 = f32[256]{0:T(256)S(1)} all-reduce(f32[256]{0:T(256)S(1)} %convert_reduce_fusion.1), channel_id=2, replica_groups=mesh['rows'=8,'rep'=4] {'rows'}, use_global_device_ids=true, to_apply=%region_4.0.clone | all-reduce | flops 256 | bytes 2048
  250.7 20.6 %reduce-scatter.2.cloned.1.call-done = f32[32,640]{1,0:T(8,128)} async-done(((f32[256,640]{1,0:T(8,128)}), f32[32,640]{1,0:T(8,128)}) %reduce-scatter.2.cloned.1.call-update) | async-done | bytes 81936 | tf_op jit(solution)/shard_map/reduce_scatter | solution.py:89
  273.9 10.1 %all_gather.3 = f32[256,640]{1,0:T(8,128)S(1)} all-gather(f32[32,640]{1,0:T(8,128)S(1)} %copy.21), channel_id=1, replica_groups=mesh['rows'=8,'rep'=4] {'rows'}, dimensions={0}, use_global_device_ids=true | all-gather | bytes 737280 | tf_op jit(solution)/shard_map/all_gather | solution.py:93
  283.9 3.2 bitcast_multiply_fusion
  288.0 34.6 %all-reduce.6.cloned.1.call-done = f32[1024,32]{0,1:T(8,128)} async-done(((f32[1024,32]{0,1:T(8,128)}), f32[1024,32]{0,1:T(8,128)}) %all-reduce.6.cloned.1.call-update) | async-done | bytes 131088 | tf_op jit(solution)/shard_map/psum | solution.py:98
  324.5 2.1 copy.22
  326.6 33.2 %all-reduce.8.cloned.1.call-done = f32[1024,32]{0,1:T(8,128)} async-done(((f32[1024,32]{0,1:T(8,128)}), f32[1024,32]{0,1:T(8,128)}) %all-reduce.8.cloned.1.call-update) | async-done | bytes 131088 | tf_op jit(solution)/shard_map/psum | solution.py:99
  (174 shorter events, 71.0 us)
Async XLA Ops:
  7.2 264.1 %reduce-scatter.2.cloned.1.call-start = ((), (), s32[]{:S(2)}) async-start(), calls=%async_computation.1 | async-start | bytes 737280 | tf_op jit(solution)/shard_map/reduce_scatter | solution.py:89
  226.1 1.6 copy-start.1
  227.7 3.4 copy-start.2
  231.0 19.6 %copy-start = (f32[640,1154]{1,0:T(8,128)}, f32[640,1154]{1,0:T(8,128)S(1)}, u32[]{:S(2)}) copy-start(f32[640,1154]{1,0:T(8,128)S(1)} %copy.19) | copy-start | bytes 8862724
  231.0 2.9 copy-start.5
  231.0 19.6 %copy-start.4 = (f32[32,4]{0,1:T(4,128)S(1)}, f32[32,4]{0,1:T(4,128)}, u32[]{:S(2)}) copy-start(f32[32,4]{0,1:T(4,128)} %param.12) | copy-start | bytes 1540
  231.0 19.6 %copy-start.3 = (f32[32,8]{0,1:T(8,128)S(1)}, f32[32,8]{0,1:T(8,128)}, u32[]{:S(2)}) copy-start(f32[32,8]{0,1:T(8,128)} %param.13) | copy-start | bytes 3076
  233.8 88.8 %all-reduce.6.cloned.1.call-start = ((), (), s32[]{:S(2)}) async-start(), calls=%async_computation.2 | async-start | bytes 262144 | tf_op jit(solution)/shard_map/psum | solution.py:98
  288.0 71.8 %all-reduce.8.cloned.1.call-start = ((), (), s32[]{:S(2)}) async-start(), calls=%async_computation.3 | async-start | bytes 262144 | tf_op jit(solution)/shard_map/psum | solution.py:99
Sparse Core Ops, SparseCore 0:
  234.0 37.2 reduce-scatter.1
  288.1 34.4 all-reduce.5
  325.6 34.1 all-reduce.7
where the time goes:
time: 371 us; the launch traced here: 368 us
  waiting for transfers between devices  88.4 us (24%)
  matrix products  76.7 us (21%)
  local copies, waits for them, and re-layouts  69 us (19%)
  other arithmetic  61.9 us (17%)
  loops' own time  31.8 us (9%)
  blocking collectives  25.2 us (7%)
  between operations  14.6 us (4%)
    dot_general x16, matrix products, add_block(): jnp.dot(spread_cells, slot_hot, preferred_element_type=jnp.float32)  69.4 us
    mul x16, other arithmetic, add_block(): weight_block[:, None, :] * cell_hot  44.4 us
    psum x1, waiting for transfers between devices, local(): centre = lax.psum(jnp.sum(shaped, axis=1), 'rep') / total_reps  34.6 us
    psum x1, waiting for transfers between devices, local(): lax.psum(jnp.sum(jnp.square(shaped - centre[:, None, :]), axis=1), 'rep')  33.2 us
    another operation x1, loops' own time, tabulate(): totals = lax.fori_loop(0, records_here // block_rows, add_block, totals)  31.8 us
    dynamic_update_slice x16, local copies, waits for them, and re-layouts, add_block(): lax.dynamic_update_slice_in_dim(totals, current + product, first_slot, 1)  30.7 us
    reduce_scatter x1, waiting for transfers between devices, local(): lax.psum_scatter(partial_value, 'rows', scatter_dimension=0, tiled=True)  20.6 us
    unnamed x1, blocking collectives  15.2 us
  transfers between devices with their start and end apart: 3, of which 3 were waited for; matrix products, arithmetic and copies ran while one was open for 1% of the time, Pallas kernels for 0%

commit v1 on v0

v1 whole, which is shorter than its diff:
```python
import jax
import jax.numpy as jnp
from jax import lax
from jax.experimental import pallas as pl
from jax.experimental.pallas import tpu as pltpu
from jax.sharding import PartitionSpec as P

AGES = 4
KINDS = 8
CELLS = 32
LOW = 32
ITERS = 4
BLOCK = 1024
HALF = CELLS // 2
TILE = 128


def rake(county_tables, groups_in, age_rate, kind_rate):
    county_rows = county_tables.shape[0]
    current = county_tables.reshape(county_rows, -1, AGES, KINDS)
    age_goal = (age_rate * groups_in[:, None])[:, None, :]
    kind_goal = (kind_rate * groups_in[:, None])[:, None, :]
    factor = jnp.ones_like(current)
    for sweep_index in range(ITERS):
        ratios = age_goal / jnp.maximum(jnp.sum(current, axis=3), 1.0)
        current = current * ratios[:, :, :, None]
        factor = factor * ratios[:, :, :, None]
        ratios = kind_goal / jnp.maximum(jnp.sum(current, axis=2), 1.0)
        current = current * ratios[:, :, None, :]
        factor = factor * ratios[:, :, None, :]
    return factor.reshape(county_rows, -1)


def exact_dot(left, right):
    return jnp.dot(left, right, precision=lax.Precision.HIGHEST, preferred_element_type=jnp.float32)


def tabulate_kernel(starts, first, low, high, weights, cells, out, group_of, total):
    tile = pl.program_id(0)
    reps = weights.shape[0]
    blocks = weights.shape[1] // BLOCK
    rows = BLOCK // 128

    @pl.when(tile == 0)
    def _():
        place0 = lax.broadcasted_iota(jnp.int32, (rows, 128), 0) * 128 + lax.broadcasted_iota(
            jnp.int32, (rows, 128), 1
        )

        def name(i, carry):
            place = place0 + i * BLOCK
            g0 = first[i]
            count = jnp.full((rows, 128), g0, jnp.int32)
            for j in range(BLOCK // LOW):
                count = count + (place >= starts[g0 + 1 + j]).astype(jnp.int32)
            group_of[pl.ds(i * rows, rows), :] = count
            return carry

        lax.fori_loop(0, blocks, name, 0)

    total[...] = jnp.zeros_like(total)
    slot = lax.broadcasted_iota(jnp.int32, (2 * TILE, 128), 0).astype(jnp.float32).astype(jnp.bfloat16)
    low_slot = lax.broadcasted_iota(jnp.int32, (HALF, 128), 0).astype(jnp.float32).astype(jnp.bfloat16)
    one = jnp.ones((2 * TILE, 128), jnp.bfloat16)
    zero = jnp.zeros((2 * TILE, 128), jnp.bfloat16)
    nothing = jnp.zeros((HALF, 128), jnp.bfloat16)

    def add_block(i, carry):
        base = pl.multiple_of(i * rows, rows)
        cell = cells[pl.ds(base, rows), :]
        near = group_of[pl.ds(base, rows), :] - tile * TILE
        inside = (near >= 0) & (near < TILE)
        place = jnp.where(inside, near + (cell // HALF) * TILE, -1).astype(jnp.float32)
        inner = (cell % HALF).astype(jnp.float32)
        lefts, rights = [], []
        for j in range(rows):
            lanes = pl.ds(pl.multiple_of(i * BLOCK + j * 128, 128), 128)
            w = weights[:, lanes].astype(jnp.float32)
            here = jnp.broadcast_to(place[j : j + 1, :], (2 * TILE, 128)).astype(jnp.bfloat16)
            rights.append(jnp.where(here == slot, one, zero))
            mask = jnp.broadcast_to(inner[j : j + 1, :], (HALF, 128)).astype(jnp.bfloat16) == low_slot
            lefts.append(
                jnp.concatenate(
                    [
                        jnp.where(
                            mask,
                            jnp.broadcast_to(w[r : r + 1, :], (HALF, 128)).astype(jnp.bfloat16),
                            nothing,
                        )
                        for r in range(reps)
                    ],
                    axis=0,
                )
            )
        left = jnp.concatenate(lefts, axis=1)
        right = jnp.concatenate(rights, axis=1)
        total[...] += lax.dot_general(
            left, right, (((1,), (1,)), ((), ())), preferred_element_type=jnp.float32
        )
        return carry

    lax.fori_loop(low[tile], high[tile], add_block, 0)
    for r in range(reps):
        for h in range(2):
            out[r * CELLS + h * HALF : r * CELLS + (h + 1) * HALF, :] = total[
                r * HALF : (r + 1) * HALF, h * TILE : (h + 1) * TILE
            ]


def tabulate(weights, cell_ids, group_sizes):
    reps, records = weights.shape
    groups = group_sizes.shape[1]
    blocks = records // BLOCK
    group_range = jnp.arange(groups, dtype=jnp.int32)
    upper = (group_range[:, None] <= group_range[None, :]).astype(jnp.float32)
    ends = exact_dot(group_sizes.astype(jnp.float32), upper)[0].astype(jnp.int32)
    starts = ends - group_sizes[0]
    edge = jnp.arange(blocks, dtype=jnp.int32) * BLOCK
    first = jnp.sum((ends[None, :] <= edge[:, None]).astype(jnp.int32), axis=1)
    low = starts[::TILE] // BLOCK
    high = (ends[TILE - 1 :: TILE] + BLOCK - 1) // BLOCK
    starts = jnp.concatenate([starts, jnp.full((128,), records + 1, jnp.int32)])
    smem = pl.BlockSpec(memory_space=pltpu.SMEM)
    return pl.pallas_call(
        tabulate_kernel,
        out_shape=jax.ShapeDtypeStruct((reps * CELLS, groups), jnp.float32),
        grid=(groups // TILE,),
        in_specs=[
            smem,
            smem,
            smem,
            smem,
            pl.BlockSpec((reps, records), lambda t: (0, 0)),
            pl.BlockSpec((records // 128, 128), lambda t: (0, 0)),
        ],
        out_specs=pl.BlockSpec((reps * CELLS, TILE), lambda t: (0, t)),
        scratch_shapes=[
            pltpu.VMEM((records // 128, 128), jnp.int32),
            pltpu.VMEM((reps * HALF, 2 * TILE), jnp.float32),
        ],
        compiler_params=pltpu.CompilerParams(vmem_limit_bytes=40 * 1024 * 1024),
    )(starts, first, low, high, weights, cell_ids.reshape(records // 128, 128))


def local(weights, cell_ids, group_sizes, group_county, age_rate, kind_rate):
    tables = tabulate(weights, cell_ids, group_sizes).T
    group_here, row_width = tables.shape
    county_ids = group_county[:, 0]
    owners = lax.axis_size("rows")
    county_here = age_rate.shape[0]
    counties = county_here * owners
    county_range = jnp.arange(counties, dtype=jnp.int32)
    county_hot = (county_ids[:, None] == county_range[None, :]).astype(jnp.float32)
    partial_value = exact_dot(county_hot.T, tables)
    member = jnp.sum(county_hot, axis=0)
    county_tables = lax.psum_scatter(partial_value, "rows", scatter_dimension=0, tiled=True)
    groups_in = lax.psum_scatter(member, "rows", scatter_dimension=0, tiled=True)
    factor = rake(county_tables, groups_in, age_rate, kind_rate)
    all_factors = lax.all_gather(factor, "rows", axis=0, tiled=True)
    raked = tables * exact_dot(county_hot, all_factors)
    reps_here = row_width // CELLS
    shaped = raked.reshape(group_here, reps_here, CELLS)
    parts = lax.axis_size("rep")
    total_reps = reps_here * parts
    mean = jnp.sum(shaped, axis=1) / reps_here
    within = jnp.sum(jnp.square(shaped - mean[:, None, :]), axis=1)
    both = lax.all_gather(jnp.stack([mean.T, within.T]), "rep", axis=0)
    means, withins = both[:, 0], both[:, 1]
    centre = jnp.sum(means, axis=0) / parts
    deviation = jnp.sum(withins + reps_here * jnp.square(means - centre[None]), axis=0)
    return (raked, deviation.T * (4.0 / total_reps))


def solution(mesh):
    placed = (
        P("rep", "rows"),
        P("rows"),
        P("rows", None),
        P("rows", None),
        P("rows", None),
        P("rows", None),
    )
    return jax.shard_map(
        local,
        mesh=mesh,
        in_specs=placed,
        out_specs=(P("rows", "rep"), P("rows", None)),
        check_vma=False,
    )
```

time: 371 us -> 142 us (0.38)
  matrix products: 76.7 us -> 7.04 us
  local copies, waits for them, and re-layouts: 69 us -> 7.42 us
  other arithmetic: 61.9 us -> 8.73 us
  waiting for transfers between devices: 88.4 us -> 46.7 us
  loops' own time: 31.8 us -> 0 us
  Pallas kernels: 0 us -> 31.6 us
    dot_general x16 -> x0, matrix products: 69.4 us -> none  [add_block(): jnp.dot(spread_cells, slot_hot, preferred_element_type=jnp.float32)]
    psum x2 -> x0, waiting for transfers between devices: 67.7 us -> none  [the longest x1 34.6 us: local(): centre = lax.psum(jnp.sum(shaped, axis=1), 'rep') / total_reps]
    mul x17 -> x2, other arithmetic: 46 us -> 0.67 us  [the longest x1 0.67 us: local(): return (raked, deviation.T * (4.0 / total_reps))]
    another operation x1 -> x0, loops' own time: 31.8 us -> none  [tabulate(): totals = lax.fori_loop(0, records_here // block_rows, add_block, totals)]
    pallas_call x0 -> x1, Pallas kernels: none -> 31.6 us  [tabulate(): pl.pallas_call(tabulate_kernel, out_shape=jax.ShapeDtypeStruct((reps * CE...]
    dynamic_update_slice x16 -> x0, local copies, waits for them, and re-layouts: 30.7 us -> none  [add_block(): lax.dynamic_update_slice_in_dim(totals, current + product, first_slot, 1)]
    dynamic_slice x64 -> x0, local copies, waits for them, and re-layouts: 29.2 us -> none  [the longest x16 15.2 us: add_block(): weight_block = lax.dynamic_slice_in_dim(weights, start, block_rows, 1)]
    all_gather x0 -> x1, waiting for transfers between devices: none -> 26 us  [local(): both = lax.all_gather(jnp.stack([mean.T, within.T]), 'rep', axis=0)]
  transfers between devices with their start and end apart: 3 -> 2, of which waited for: 3 -> 2; matrix products, arithmetic and copies ran while one was open for 1% -> 2% of each run, Pallas kernels for 0% -> 0%
where the time goes in v1:
time: 142 us
  waiting for transfers between devices  46.7 us (33%)
  Pallas kernels  31.6 us (22%)
  blocking collectives  25.2 us (18%)
  between operations  14.9 us (10%)
  other arithmetic  8.73 us (6%)
  local copies, waits for them, and re-layouts  7.42 us (5%)
  matrix products  7.04 us (5%)
    pallas_call x1, Pallas kernels, tabulate(): pl.pallas_call(tabulate_kernel, out_shape=jax.ShapeDtypeStruct((reps * CE...  31.6 us
    all_gather x1, waiting for transfers between devices, local(): both = lax.all_gather(jnp.stack([mean.T, within.T]), 'rep', axis=0)  26 us
    reduce_scatter x1, waiting for transfers between devices, local(): lax.psum_scatter(partial_value, 'rows', scatter_dimension=0, tiled=True)  20.6 us
    unnamed x1, blocking collectives  15.1 us
    all_gather x1, blocking collectives, local(): all_factors = lax.all_gather(factor, 'rows', axis=0, tiled=True)  10.1 us
    dot_general x3, matrix products, exact_dot(): jnp.dot(left, right, precision=lax.Precision.HIGHEST, preferred_element_t...  7.04 us
    unnamed x17, local copies, waits for them, and re-layouts  6.06 us
  transfers between devices with their start and end apart: 2, of which 2 were waited for; matrix products, arithmetic and copies ran while one was open for 2% of the time, Pallas kernels for 0%

profile of v1, /device:TPU:0, one launch (start us, length us, event | category | flops | bytes accessed | tf_op | source)
XLA Modules:
  0.0 141.7 jit_solution(7150523782041688299)
XLA Ops:
  7.2 0.0 reduce-scatter.2.cloned.1.call-start
  7.2 1.3 fusion
  8.6 0.7 convert_subtract_fusion
  9.3 0.1 slice.13
  9.4 0.2 convert_reduce_fusion.1.first
  9.6 0.1 slice.12
  9.7 0.0 copy-start
  9.7 1.9 %copy-done = bf16[20,65536]{1,0:T(8,128)(2,1)S(1)} copy-done((bf16[20,65536]{1,0:T(8,128)(2,1)S(1)}, bf16[20,65536]{1,0:T(8,128)(2,1)}, u32[]{:S(2)}) %copy-start) | copy-done | bytes 2621464
  11.6 0.9 copy-done.1
  12.5 31.6 %shard_map.77 = f32[640,1024]{1,0:T(8,128)S(1)} custom-call(s32[1152]{0:T(1024)S(1)} %concatenate.3.starts, s32[64]{0:T(128)S(1)} %convert_reduce_fusion.1.first, s32[8]{0:T(128)S(1)} %get-tuple-element.13.low, s32[8]{0:T(128)S(1)} %get-tuple-element.12.high, bf16[20,65536]{1,0:T(8,128)(2,1)S(1)} %copy-done, s32[512,128]{1,0:T(8,128)S(1)} %bitcast.42), custom_call_target="tpu_custom_call" | custom-call | tf_op jit(solution)/shard_map/pallas_call | solution.py:124
  44.2 0.0 copy-start.6
  44.2 0.0 copy-start.5
  44.2 0.0 copy-start.4
  44.2 0.0 copy-done.3
  44.2 2.7 %fusion.2 = f32[256,640]{1,0:T(8,128)} fusion(f32[640,1024]{1,0:T(8,128)S(1)} %shard_map.77, s32[1024]{0:T(1024)S(1)} %bitcast.57), kind=kOutput, calls=%fused_computation.7 | convolution fusion | flops 2013790208 | bytes 3280896 | tf_op jit(solution)/shard_map/dot_general | solution.py:35
  47.0 0.0 reduce-scatter.2.cloned.1.call-update
  47.0 0.0 all-gather.3.cloned.1.call-start
  47.0 0.0 copy-done.6
  47.0 0.6 dynamic-slice
  48.3 0.2 convert_reduce_fusion
  48.5 15.1 %all-reduce.1 = f32[256]{0:T(256)S(1)} all-reduce(f32[256]{0:T(256)S(1)} %convert_reduce_fusion), channel_id=3, replica_groups=mesh['rows'=8,'rep'=4] {'rows'}, use_global_device_ids=true, to_apply=%region_2.3.clone | all-reduce | flops 256 | bytes 2048
  63.6 0.1 dynamic-slice.1
  63.7 0.0 copy-done.5
  63.7 0.0 copy-done.4
  63.7 20.6 %reduce-scatter.2.cloned.1.call-done = f32[32,640]{1,0:T(8,128)} async-done(((f32[256,640]{1,0:T(8,128)}), f32[32,640]{1,0:T(8,128)}) %reduce-scatter.2.cloned.1.call-update) | async-done | bytes 81936 | tf_op jit(solution)/shard_map/reduce_scatter | solution.py:156
  84.4 1.0 copy.19
  85.4 0.1 reduce_sum.128
  85.6 0.1 multiply_reduce_fusion.5
  85.6 0.2 multiply_reduce_fusion.4
  85.8 0.1 fusion.14
  85.9 0.2 multiply_reduce_fusion.3
  86.1 0.1 fusion.10
  86.3 0.2 multiply_reduce_fusion.2
  86.6 0.2 multiply_reduce_fusion.1
  86.7 0.1 multiply_multiply_fusion
  86.9 0.1 copy.20
  87.0 10.1 %all_gather.9 = f32[256,640]{1,0:T(8,128)S(1)} all-gather(f32[32,640]{1,0:T(8,128)S(1)} %copy.20), channel_id=1, replica_groups=mesh['rows'=8,'rep'=4] {'rows'}, dimensions={0}, use_global_device_ids=true | all-gather | bytes 737280 | tf_op jit(solution)/shard_map/all_gather | solution.py:159
  97.1 2.9 %bitcast_multiply_fusion = f32[1024,640]{0,1:T(8,128)} fusion(f32[640,1024]{1,0:T(8,128)S(1)} %shard_map.77, f32[256,640]{1,0:T(8,128)S(1)} %all_gather.9, s32[1024]{0:T(1024)S(1)} %bitcast.59), kind=kOutput, calls=%fused_computation.2 | convolution fusion | flops 2014183424 | bytes 5902336 | tf_op jit(solution)/shard_map/dot_general | solution.py:35
  100.0 2.0 %reduce_sum.136 = f32[1024,32]{0,1:T(8,128)S(1)} reduce(f32[1024,20,32]{0,2,1:T(8,128)} %bitcast.43, f32[]{:T(128)} %constant.41.clone.1), dimensions={1}, to_apply=%region_12.13 | reduce | flops 622592 | bytes 2752516 | tf_op jit(solution)/shard_map/reduce_sum | solution.py:165
  102.1 0.5 copy-done.2
  102.6 0.3 multiply_reduce_fusion
  102.9 0.7 pad_maximum_fusion
  103.6 0.0 all-gather.3.cloned.1.call-update
  103.6 2.1 %copy.22 = f32[1024,640]{1,0:T(8,128)} copy(f32[1024,640]{0,1:T(8,128)S(1)} %copy-done.2) | data formatting | bytes 5242880
  105.7 26.0 %all-gather.3.cloned.1.call-done = f32[8,32,1024]{2,1,0:T(8,128)} async-done(((f32[2,32,1024]{2,1,0:T(8,128)}), f32[8,32,1024]{2,1,0:T(8,128)}) %all-gather.3.cloned.1.call-update) | async-done | bytes 1048592 | tf_op jit(solution)/shard_map/all_gather | solution.py:167
  131.7 1.1 slice_reduce_fusion
  132.8 1.3 fusion.5
  134.2 0.7 multiply_bitcast_fusion
  (19 shorter events, 0.2 us)
Async XLA Ops:
  7.2 77.2 %reduce-scatter.2.cloned.1.call-start = ((), (), s32[]{:S(2)}) async-start(), calls=%async_computation.1 | async-start | bytes 737280 | tf_op jit(solution)/shard_map/reduce_scatter | solution.py:156
  9.7 1.9 %copy-start = (bf16[20,65536]{1,0:T(8,128)(2,1)S(1)}, bf16[20,65536]{1,0:T(8,128)(2,1)}, u32[]{:S(2)}) copy-start(bf16[20,65536]{1,0:T(8,128)(2,1)} %weights.1) | copy-start | bytes 7864324
  11.6 0.9 copy-start.1
  12.5 31.7 %copy-start.3 = (s32[1024,1]{0,1:T(1,128)S(1)}, s32[1024,1]{0,1:T(1,128)}, u32[]{:S(2)}) copy-start(s32[1024,1]{0,1:T(1,128)} %param.9) | copy-start | bytes 12292
  44.2 2.9 %copy-start.6 = (u32[32]{0:T(128)S(1)}, u32[32]{0:T(128)}, u32[]{:S(2)}) copy-start(u32[32]{0:T(128)} %constant.51) | copy-start | bytes 388
  44.2 19.5 %copy-start.5 = (f32[32,4]{0,1:T(4,128)S(1)}, f32[32,4]{0,1:T(4,128)}, u32[]{:S(2)}) copy-start(f32[32,4]{0,1:T(4,128)} %param.10) | copy-start | bytes 1540
  44.2 19.5 %copy-start.4 = (f32[32,8]{0,1:T(8,128)S(1)}, f32[32,8]{0,1:T(8,128)}, u32[]{:S(2)}) copy-start(f32[32,8]{0,1:T(8,128)} %param.11) | copy-start | bytes 3076
  47.0 84.8 %all-gather.3.cloned.1.call-start = ((), (), s32[]{:S(2)}) async-start(), calls=%async_computation.2 | async-start | bytes 1310720 | tf_op jit(solution)/shard_map/all_gather | solution.py:167
  100.0 2.5 %copy-start.2 = (f32[1024,640]{0,1:T(8,128)S(1)}, f32[1024,640]{0,1:T(8,128)}, u32[]{:S(2)}) copy-start(f32[1024,640]{0,1:T(8,128)} %bitcast_multiply_fusion) | copy-start | bytes 7864324
Sparse Core Ops, SparseCore 0:
  47.1 37.2 reduce-scatter.1
  103.8 27.9 all-gather.2

commit v2 on v1

--- a/solution.py
+++ b/solution.py
@@ -1,3 +1,5 @@
+import functools
+
 import jax
 import jax.numpy as jnp
 from jax import lax
@@ -13,22 +15,7 @@
 BLOCK = 1024
 HALF = CELLS // 2
 TILE = 128
-
-
-def rake(county_tables, groups_in, age_rate, kind_rate):
-    county_rows = county_tables.shape[0]
-    current = county_tables.reshape(county_rows, -1, AGES, KINDS)
-    age_goal = (age_rate * groups_in[:, None])[:, None, :]
-    kind_goal = (kind_rate * groups_in[:, None])[:, None, :]
-    factor = jnp.ones_like(current)
-    for sweep_index in range(ITERS):
-        ratios = age_goal / jnp.maximum(jnp.sum(current, axis=3), 1.0)
-        current = current * ratios[:, :, :, None]
-        factor = factor * ratios[:, :, :, None]
-        ratios = kind_goal / jnp.maximum(jnp.sum(current, axis=2), 1.0)
-        current = current * ratios[:, :, None, :]
-        factor = factor * ratios[:, :, None, :]
-    return factor.reshape(county_rows, -1)
+MESH = pl.DeviceIdType.MESH
 
 
 def exact_dot(left, right):
@@ -142,33 +129,226 @@
     )(starts, first, low, high, weights, cell_ids.reshape(records // 128, 128))
 
 
+def pieces(value):
+    upper = value.astype(jnp.bfloat16)
+    lower = (value - upper.astype(jnp.float32)).astype(jnp.bfloat16)
+    return upper, lower
+
+
+def rake(columns, goals, reps):
+    cells = columns[: reps * CELLS, :].reshape(reps, AGES, KINDS, 128)
+    member = columns[reps * CELLS : reps * CELLS + 8, :]
+    ages = [(goals[a : a + 1, :] * member[0:1, :]).reshape(1, 1, 128) for a in range(AGES)]
+    kinds = (goals[8:16, :] * member).reshape(1, KINDS, 128)
+    current = [cells[:, a] for a in range(AGES)]
+    by_age = [jnp.ones((reps, 1, 128), jnp.float32) for _ in range(AGES)]
+    by_kind = jnp.ones((reps, KINDS, 128), jnp.float32)
+    for _ in range(ITERS):
+        for a in range(AGES):
+            ratio = ages[a] / jnp.maximum(jnp.sum(current[a], axis=1, keepdims=True), 1.0)
+            current[a] = current[a] * ratio
+            by_age[a] = by_age[a] * ratio
+        ratio = kinds / jnp.maximum(current[0] + current[1] + current[2] + current[3], 1.0)
+        current = [c * ratio for c in current]
+        by_kind = by_kind * ratio
+    row = lax.broadcasted_iota(jnp.int32, (reps, 8, 128), 1)
+    ages_full = jnp.broadcast_to(by_age[3], (reps, 8, 128))
+    for a in range(AGES - 1):
+        ages_full = jnp.where(row == a, by_age[a], ages_full)
+    return jnp.concatenate([ages_full, by_kind], axis=1).reshape(reps * 16, 128)
+
+
+def finish_kernel(
+    owners, parts, tables, county, goals, raked, spread,
+    hot, partial, inbox, factors, picked, moments, arrived, shares,
+    sum_send, sum_recv, factor_send, factor_recv, part_send, part_recv, share_send, share_recv,
+):
+    me = lax.axis_index("rows")
+    mine = lax.axis_index("rep")
+    width, groups = tables.shape
+    reps = width // CELLS
+    counties = hot.shape[0]
+    here = counties // owners
+    quarter = groups // parts
+    barrier = pltpu.get_barrier_semaphore()
+    for d in range(1, owners):
+        pl.semaphore_signal(barrier, inc=1, device_id={"rows": lax.rem(me + d, owners)}, device_id_type=MESH)
+    for d in range(1, parts):
+        pl.semaphore_signal(barrier, inc=1, device_id={"rep": lax.rem(mine + d, parts)}, device_id_type=MESH)
+
+    ids = lax.broadcasted_iota(jnp.int32, (counties, groups), 0)
+    is_member = (ids == jnp.broadcast_to(county[...], (counties, groups))).astype(jnp.float32)
+    hot[...] = is_member.astype(jnp.bfloat16)
+    partial[:, width:] = jnp.broadcast_to(jnp.sum(is_member, axis=1, keepdims=True), (counties, 128))
+    upper, lower = pieces(tables[...])
+    contract = (((1,), (1,)), ((), ()))
+    partial[:, :width] = lax.dot_general(
+        hot[...], upper, contract, preferred_element_type=jnp.float32
+    ) + lax.dot_general(hot[...], lower, contract, preferred_element_type=jnp.float32)
+    pl.semaphore_wait(barrier, owners - 1 + parts - 1)
+
+    def rows_of(owner):
+        return pl.ds(pl.multiple_of(owner * here, here), here)
+
+    def lanes_of(part):
+        return pl.ds(pl.multiple_of(part * quarter, quarter), quarter)
+
+    sums = []
+    for d in range(1, owners):
+        target = lax.rem(me + d, owners)
+        copy = pltpu.make_async_remote_copy(
+            src_ref=partial.at[rows_of(target)],
+            dst_ref=inbox.at[d - 1],
+            send_sem=sum_send.at[d - 1],
+            recv_sem=sum_recv.at[d - 1],
+            device_id={"rows": target},
+            device_id_type=MESH,
+        )
+        copy.start()
+        sums.append(copy)
+    total = partial[rows_of(me), :]
+    for d in range(1, owners):
+        sums[d - 1].wait_recv()
+        total = total + inbox[d - 1]
+    columns = jnp.concatenate([total, jnp.zeros((128 - here, width + 128), jnp.float32)], axis=0).T
+    found = rake(columns, goals[...], reps)
+    room = factors.shape[1]
+    found = jnp.concatenate([found, jnp.zeros((room - reps * 16, 128), jnp.float32)], axis=0)
+    factors[rows_of(me), :] = found.T[:here, :]
+    gathers = []
+    for d in range(1, owners):
+        target = lax.rem(me + d, owners)
+        copy = pltpu.make_async_remote_copy(
+            src_ref=factors.at[rows_of(me)],
+            dst_ref=factors.at[rows_of(me)],
+            send_sem=factor_send.at[d - 1],
+            recv_sem=factor_recv.at[d - 1],
+            device_id={"rows": target},
+            device_id_type=MESH,
+        )
+        copy.start()
+        gathers.append(copy)
+    for copy in gathers:
+        copy.wait_recv()
+    upper, lower = pieces(factors[...].T)
+    picked[...] = jnp.dot(upper, hot[...], preferred_element_type=jnp.float32) + jnp.dot(
+        lower, hot[...], preferred_element_type=jnp.float32
+    )
+
+    def work(part):
+        for t in range(quarter // 128):
+            lanes = pl.ds(pl.multiple_of(part * quarter + t * 128, 128), 128)
+            inner = pl.ds(t * 128, 128)
+            count = [jnp.zeros((8, 128), jnp.float32) for _ in range(AGES)]
+            for r in range(reps):
+                by_age = picked[r * 16 : r * 16 + 8, lanes]
+                by_kind = picked[r * 16 + 8 : r * 16 + 16, lanes]
+                for a in range(AGES):
+                    at = r * CELLS + a * 8
+                    value = tables[at : at + 8, lanes] * (by_kind * by_age[a : a + 1, :])
+                    raked[at : at + 8, lanes] = value
+                    count[a] = count[a] + value
+            for a in range(AGES):
+                mean = count[a] / reps
+                within = jnp.zeros((8, 128), jnp.float32)
+                for r in range(reps):
+                    at = r * CELLS + a * 8
+                    within = within + jnp.square(raked[at : at + 8, lanes] - mean)
+                moments[part, a * 8 : a * 8 + 8, inner] = mean
+                moments[part, CELLS + a * 8 : CELLS + a * 8 + 8, inner] = within
+
+    sends = []
+    for d in range(1, parts):
+        target = lax.rem(mine + d, parts)
+        work(target)
+        copy = pltpu.make_async_remote_copy(
+            src_ref=moments.at[target],
+            dst_ref=arrived.at[d - 1],
+            send_sem=part_send.at[d - 1],
+            recv_sem=part_recv.at[d - 1],
+            device_id={"rep": target},
+            device_id_type=MESH,
+        )
+        copy.start()
+        sends.append(copy)
+    work(mine)
+    own = moments[mine]
+    both = [own]
+    for d in range(1, parts):
+        sends[d - 1].wait_recv()
+        both.append(arrived[d - 1])
+    centre = both[0][:CELLS]
+    for other in both[1:]:
+        centre = centre + other[:CELLS]
+    centre = centre / parts
+    deviation = jnp.zeros((CELLS, quarter), jnp.float32)
+    for other in both:
+        deviation = deviation + (other[CELLS:] + reps * jnp.square(other[:CELLS] - centre))
+    shares[mine] = deviation * (4.0 / (reps * parts))
+    answers = []
+    for d in range(1, parts):
+        target = lax.rem(mine + d, parts)
+        copy = pltpu.make_async_remote_copy(
+            src_ref=shares.at[mine],
+            dst_ref=shares.at[mine],
+            send_sem=share_send.at[d - 1],
+            recv_sem=share_recv.at[d - 1],
+            device_id={"rep": target},
+            device_id_type=MESH,
+        )
+        copy.start()
+        answers.append(copy)
+    for copy in answers:
+        copy.wait_recv()
+    for part in range(parts):
+        spread[:, part * quarter : (part + 1) * quarter] = shares[part]
+    for copy in sums + gathers + sends + answers:
+        copy.wait_send()
+
+
 def local(weights, cell_ids, group_sizes, group_county, age_rate, kind_rate):
-    tables = tabulate(weights, cell_ids, group_sizes).T
-    group_here, row_width = tables.shape
-    county_ids = group_county[:, 0]
-    owners = lax.axis_size("rows")
-    county_here = age_rate.shape[0]
-    counties = county_here * owners
-    county_range = jnp.arange(counties, dtype=jnp.int32)
-    county_hot = (county_ids[:, None] == county_range[None, :]).astype(jnp.float32)
-    partial_value = exact_dot(county_hot.T, tables)
-    member = jnp.sum(county_hot, axis=0)
-    county_tables = lax.psum_scatter(partial_value, "rows", scatter_dimension=0, tiled=True)
-    groups_in = lax.psum_scatter(member, "rows", scatter_dimension=0, tiled=True)
-    factor = rake(county_tables, groups_in, age_rate, kind_rate)
-    all_factors = lax.all_gather(factor, "rows", axis=0, tiled=True)
-    raked = tables * exact_dot(county_hot, all_factors)
-    reps_here = row_width // CELLS
-    shaped = raked.reshape(group_here, reps_here, CELLS)
-    parts = lax.axis_size("rep")
-    total_reps = reps_here * parts
-    mean = jnp.sum(shaped, axis=1) / reps_here
-    within = jnp.sum(jnp.square(shaped - mean[:, None, :]), axis=1)
-    both = lax.all_gather(jnp.stack([mean.T, within.T]), "rep", axis=0)
-    means, withins = both[:, 0], both[:, 1]
-    centre = jnp.sum(means, axis=0) / parts
-    deviation = jnp.sum(withins + reps_here * jnp.square(means - centre[None]), axis=0)
-    return (raked, deviation.T * (4.0 / total_reps))
+    owners, parts = lax.axis_size("rows"), lax.axis_size("rep")
+    tables = tabulate(weights, cell_ids, group_sizes)
+    width, groups = tables.shape
+    here = age_rate.shape[0]
+    counties = here * owners
+    room = -(-(width // 2) // 128) * 128
+    goals = jnp.concatenate([age_rate.T, jnp.zeros((8 - AGES, here), jnp.float32), kind_rate.T], axis=0)
+    goals = jnp.pad(goals, ((0, 0), (0, 128 - here)))
+    quarter = groups // parts
+    vmem = pl.BlockSpec(memory_space=pltpu.VMEM)
+    dma = pltpu.SemaphoreType.DMA
+    raked, spread = pl.pallas_call(
+        functools.partial(finish_kernel, owners, parts),
+        out_shape=(
+            jax.ShapeDtypeStruct((width, groups), jnp.float32),
+            jax.ShapeDtypeStruct((CELLS, groups), jnp.float32),
+        ),
+        in_specs=[vmem] * 3,
+        out_specs=(vmem, vmem),
+        scratch_shapes=[
+            pltpu.VMEM((counties, groups), jnp.bfloat16),
+            pltpu.VMEM((counties, width + 128), jnp.float32),
+            pltpu.VMEM((owners - 1, here, width + 128), jnp.float32),
+            pltpu.VMEM((counties, room), jnp.float32),
+            pltpu.VMEM((room, groups), jnp.float32),
+            pltpu.VMEM((parts, 2 * CELLS, quarter), jnp.float32),
+            pltpu.VMEM((parts - 1, 2 * CELLS, quarter), jnp.float32),
+            pltpu.VMEM((parts, CELLS, quarter), jnp.float32),
+            dma((owners - 1,)),
+            dma((owners - 1,)),
+            dma((owners - 1,)),
+            dma((owners - 1,)),
+            dma((parts - 1,)),
+            dma((parts - 1,)),
+            dma((parts - 1,)),
+            dma((parts - 1,)),
+        ],
+        compiler_params=pltpu.CompilerParams(
+            collective_id=0, has_side_effects=True, vmem_limit_bytes=48 * 1024 * 1024
+        ),
+    )(tables, group_county.reshape(1, groups), goals)
+    return raked.T, spread.T
 
 
 def solution(mesh):

time: 142 us -> 77 us (0.54)
  waiting for transfers between devices: 46.7 us -> 0 us
  Pallas kernels: 31.6 us -> 67.2 us
  blocking collectives: 25.2 us -> 0 us
  between operations: 14.9 us -> 0.68 us
  other arithmetic: 8.73 us -> 1.7 us
  matrix products: 7.04 us -> 1.34 us
  local copies, waits for them, and re-layouts: 7.42 us -> 5.85 us
    pallas_call x0 -> x1, Pallas kernels: none -> 35.5 us  [local(): pl.pallas_call(functools.partial(finish_kernel, owners, parts), out_shape...]
    all_gather x1 -> x0, waiting for transfers between devices: 26 us -> none  [local(): both = lax.all_gather(jnp.stack([mean.T, within.T]), 'rep', axis=0)]
    reduce_scatter x1 -> x0, waiting for transfers between devices: 20.6 us -> none  [local(): lax.psum_scatter(partial_value, 'rows', scatter_dimension=0, tiled=True)]
    unnamed x1 -> x0, blocking collectives: 15.1 us -> none
    all_gather x1 -> x0, blocking collectives: 10.1 us -> none  [local(): all_factors = lax.all_gather(factor, 'rows', axis=0, tiled=True)]
    reduce_sum x13 -> x0, other arithmetic: 6.08 us -> none  [the longest x1 2.04 us: local(): mean = jnp.sum(shaped, axis=1) / reps_here]
    dot_general x3 -> x1, matrix products: 7.04 us -> 1.34 us  [exact_dot(): jnp.dot(left, right, precision=lax.Precision.HIGHEST, preferred_element_t...]
    unnamed x17 -> x8, local copies, waits for them, and re-layouts: 6.06 us -> 5.59 us
  transfers between devices with their start and end apart: 2 -> 0, of which waited for: 2 -> 0; matrix products, arithmetic and copies ran while one was open for 2% -> 0% of each run, Pallas kernels for 0% -> 0%
where the time goes in v2:
time: 77 us; the launch traced here: 76.8 us
  Pallas kernels  67.2 us (87%)
  local copies, waits for them, and re-layouts  5.85 us (8%)
  other arithmetic  1.7 us (2%)
  matrix products  1.34 us (2%)
    pallas_call x1, Pallas kernels, local(): pl.pallas_call(functools.partial(finish_kernel, owners, parts), out_shape...  35.5 us
    pallas_call x1, Pallas kernels, tabulate(): pl.pallas_call(tabulate_kernel, out_shape=jax.ShapeDtypeStruct((reps * CE...  31.6 us
    unnamed x8, local copies, waits for them, and re-layouts  5.59 us

profile of v2, /device:TPU:0, one launch (start us, length us, event | category | flops | bytes accessed | tf_op | source)
XLA Modules:
  0.0 76.8 jit_solution(1922493947539525820)
XLA Ops:
  0.6 0.1 pad.7.clone
  0.7 1.3 %fusion = f32[1,1024]{1,0:T(1,128)S(1)} fusion(s32[1,1024]{1,0:T(1,128)} %param.8), kind=kOutput, calls=%fused_computation.1 | convolution fusion | flops 13632512 | bytes 8192 | tf_op jit(solution)/shard_map/dot_general | solution.py:22
  2.1 0.0 copy-start.2
  2.1 0.7 convert_subtract_fusion
  2.8 0.2 convert_reduce_fusion.first
  3.0 0.1 slice.7
  3.1 0.1 slice.6
  3.2 0.8 %pad_maximum_fusion = f32[16,32]{1,0:T(8,128)S(1)} fusion(f32[8,32]{1,0:T(8,128)} %bitcast.19, f32[4,32]{1,0:T(4,128)} %bitcast.20, f32[16]{0:T(128)S(1)} %pad.7.clone), kind=kLoop, calls=%fused_computation.3 | loop fusion | flops 1024 | bytes 3648 | tf_op jit(solution)/shard_map/concatenate | solution.py:316
  4.0 0.0 copy-start
  4.0 1.9 %copy-done = bf16[20,65536]{1,0:T(8,128)(2,1)S(1)} copy-done((bf16[20,65536]{1,0:T(8,128)(2,1)S(1)}, bf16[20,65536]{1,0:T(8,128)(2,1)}, u32[]{:S(2)}) %copy-start) | copy-done | bytes 2621464
  5.9 0.0 copy-start.1
  5.9 0.9 %copy-done.1 = s32[65536]{0:T(1024)S(1)} copy-done((s32[65536]{0:T(1024)S(1)}, s32[65536]{0:T(1024)}, u32[]{:S(2)}) %copy-start.1) | copy-done | bytes 262168
  6.8 31.6 %shard_map.77.tables = f32[640,1024]{1,0:T(8,128)S(1)} custom-call(s32[1152]{0:T(1024)S(1)} %concatenate.6.starts, s32[64]{0:T(128)S(1)} %convert_reduce_fusion.first, s32[8]{0:T(128)S(1)} %get-tuple-element.11.low, s32[8]{0:T(128)S(1)} %get-tuple-element.10.high, bf16[20,65536]{1,0:T(8,128)(2,1)S(1)} %copy-done, s32[512,128]{1,0:T(8,128)S(1)} %bitcast.13), custom_call_target="tpu_custom_call" | custom-call | tf_op jit(solution)/shard_map/pallas_call | solution.py:111
  38.5 0.0 copy-done.2
  38.5 35.5 %shard_map.78 = (f32[640,1024]{1,0:T(8,128)S(1)}, f32[32,1024]{1,0:T(8,128)S(1)}) custom-call(f32[640,1024]{1,0:T(8,128)S(1)} %shard_map.77.tables, s32[1,1024]{1,0:T(1,128)S(1)} %bitcast.15, f32[16,128]{1,0:T(8,128)S(1)} %pad.5.goals), custom_call_target="tpu_custom_call" | custom-call | tf_op jit(solution)/shard_map/pallas_call | solution.py:321
  74.0 2.1 %copy.9 = f32[1024,640]{1,0:T(8,128)} copy(f32[1024,640]{0,1:T(8,128)S(1)} %bitcast.12) | data formatting | bytes 5242880
  76.1 0.7 copy.11
  (6 shorter events, 0.0 us)
Async XLA Ops:
  2.1 36.4 %copy-start.2 = (s32[1024,1]{0,1:T(1,128)S(1)}, s32[1024,1]{0,1:T(1,128)}, u32[]{:S(2)}) copy-start(s32[1024,1]{0,1:T(1,128)} %param.9) | copy-start | bytes 12292
  4.0 1.9 %copy-start = (bf16[20,65536]{1,0:T(8,128)(2,1)S(1)}, bf16[20,65536]{1,0:T(8,128)(2,1)}, u32[]{:S(2)}) copy-start(bf16[20,65536]{1,0:T(8,128)(2,1)} %weights.1) | copy-start | bytes 7864324
  5.9 0.9 %copy-start.1 = (s32[65536]{0:T(1024)S(1)}, s32[65536]{0:T(1024)}, u32[]{:S(2)}) copy-start(s32[65536]{0:T(1024)} %param.7) | copy-start | bytes 786436

commit v3 on v2

v3 whole, which is shorter than its diff:
```python
import functools

import jax
import jax.numpy as jnp
from jax import lax
from jax.experimental import pallas as pl
from jax.experimental.pallas import tpu as pltpu
from jax.sharding import PartitionSpec as P

AGES = 4
KINDS = 8
CELLS = 32
LOW = 32
ITERS = 4
UNIT = 1024
STEP = 3
CUT = 12
HALF = CELLS // 2
TILE = 128
MESH = pl.DeviceIdType.MESH


def exact_dot(left, right):
    return jnp.dot(left, right, precision=lax.Precision.HIGHEST, preferred_element_type=jnp.float32)


def tabulate_kernel(starts, first, weights, cells, out, columns, inners):
    reps, records = weights.shape
    groups = out.shape[1]
    out[...] = jnp.zeros_like(out)
    slot = lax.broadcasted_iota(jnp.int32, (2 * TILE, 128), 0).astype(jnp.float32).astype(jnp.bfloat16)
    low_slot = lax.broadcasted_iota(jnp.int32, (HALF, 128), 0).astype(jnp.float32).astype(jnp.bfloat16)
    one = jnp.ones((2 * TILE, 128), jnp.bfloat16)
    zero = jnp.zeros((2 * TILE, 128), jnp.bfloat16)
    nothing = jnp.zeros((HALF, 128), jnp.bfloat16)
    place0 = lax.broadcasted_iota(jnp.int32, (8, 128), 0) * 128 + lax.broadcasted_iota(jnp.int32, (8, 128), 1)
    lane = lax.broadcasted_iota(jnp.int32, (reps * HALF, TILE), 1)

    def name(at, carry):
        place = place0 + at * UNIT
        g0 = first[at]
        counts = [jnp.full((8, 128), g0, jnp.int32)] + [jnp.zeros((8, 128), jnp.int32)] * 3
        for j in range(UNIT // LOW):
            counts[j % 4] = counts[j % 4] + (place >= starts[g0 + 1 + j]).astype(jnp.int32)
        count = (counts[0] + counts[1]) + (counts[2] + counts[3])
        rows = pl.ds(pl.multiple_of(at * 8, 8), 8)
        cell = cells[rows, :]
        columns[rows, :] = (count % TILE + (cell // HALF) * TILE).astype(jnp.float32)
        inners[rows, :] = (cell % HALF).astype(jnp.float32)
        return carry

    lax.fori_loop(0, records // UNIT, name, 0, unroll=2)

    def add_block(unit, units):
        lefts, rights = [], []
        for u in range(units):
            at = unit + u
            column = columns[pl.ds(pl.multiple_of(at * 8, 8), 8), :]
            inner = inners[pl.ds(pl.multiple_of(at * 8, 8), 8), :]
            for j in range(8):
                lanes = pl.ds(pl.multiple_of(at * UNIT + j * 128, 128), 128)
                w = weights[:, lanes].astype(jnp.float32)
                here = jnp.broadcast_to(column[j : j + 1, :], (2 * TILE, 128)).astype(jnp.bfloat16)
                rights.append(jnp.where(here == slot, one, zero))
                mask = jnp.broadcast_to(inner[j : j + 1, :], (HALF, 128)).astype(jnp.bfloat16) == low_slot
                lefts.append(
                    jnp.concatenate(
                        [
                            jnp.where(
                                mask,
                                jnp.broadcast_to(w[r : r + 1, :], (HALF, 128)).astype(jnp.bfloat16),
                                nothing,
                            )
                            for r in range(reps)
                        ],
                        axis=0,
                    )
                )
        found = lax.dot_general(
            jnp.concatenate(lefts, axis=1),
            jnp.concatenate(rights, axis=1),
            (((1,), (1,)), ((), ())),
            preferred_element_type=jnp.float32,
        )
        g0 = first[unit]
        tile = g0 // TILE
        following = jnp.minimum(tile + 1, groups // TILE - 1)
        wrapped = lane < g0 % TILE
        for h in range(2):
            half = found[:, h * TILE : (h + 1) * TILE]
            for where, part in (
                (tile, jnp.where(wrapped, 0.0, half)),
                (following, jnp.where(wrapped, half, 0.0)),
            ):
                lanes = pl.ds(pl.multiple_of(where * TILE, TILE), TILE)
                for r in range(reps):
                    at = r * CELLS + h * HALF
                    out[at : at + HALF, lanes] += part[r * HALF : (r + 1) * HALF, :]

    units = records // UNIT
    whole = units // STEP

    def step(i, carry):
        add_block(i * STEP, STEP)
        return carry

    lax.fori_loop(0, whole, step, 0)
    if units % STEP:
        add_block(whole * STEP, units % STEP)


def tabulate(weights, cell_ids, group_sizes):
    reps, records = weights.shape
    groups = group_sizes.shape[1]
    group_range = jnp.arange(groups, dtype=jnp.int32)
    upper = (group_range[:, None] <= group_range[None, :]).astype(jnp.float32)
    ends = exact_dot(group_sizes.astype(jnp.float32), upper)[0].astype(jnp.int32)
    starts = ends - group_sizes[0]
    edge = jnp.arange(records // UNIT, dtype=jnp.int32) * UNIT
    first = jnp.sum((ends[None, :] <= edge[:, None]).astype(jnp.int32), axis=1)
    starts = jnp.concatenate([starts, jnp.full((128,), records + 1, jnp.int32)])
    smem = pl.BlockSpec(memory_space=pltpu.SMEM)
    vmem = pl.BlockSpec(memory_space=pltpu.VMEM)
    return pl.pallas_call(
        tabulate_kernel,
        out_shape=jax.ShapeDtypeStruct((reps * CELLS, groups), jnp.float32),
        in_specs=[smem, smem, vmem, vmem],
        out_specs=vmem,
        scratch_shapes=[pltpu.VMEM((records // 128, 128), jnp.float32)] * 2,
        compiler_params=pltpu.CompilerParams(vmem_limit_bytes=40 * 1024 * 1024),
    )(starts, first, weights, cell_ids.reshape(records // 128, 128))


def pieces(value):
    upper = value.astype(jnp.bfloat16)
    lower = (value - upper.astype(jnp.float32)).astype(jnp.bfloat16)
    return upper, lower


def rake(columns, member, goals):
    reps = columns.shape[0] // CELLS
    cells = columns.reshape(reps, AGES, KINDS, 128)
    ages = [(goals[a : a + 1, :] * member[0:1, :]).reshape(1, 1, 128) for a in range(AGES)]
    kinds = (goals[8:16, :] * member).reshape(1, KINDS, 128)
    current = [cells[:, a] for a in range(AGES)]
    by_age = [jnp.ones((reps, 1, 128), jnp.float32) for _ in range(AGES)]
    by_kind = jnp.ones((reps, KINDS, 128), jnp.float32)
    for _ in range(ITERS):
        for a in range(AGES):
            ratio = ages[a] / jnp.maximum(jnp.sum(current[a], axis=1, keepdims=True), 1.0)
            current[a] = current[a] * ratio
            by_age[a] = by_age[a] * ratio
        ratio = kinds / jnp.maximum(current[0] + current[1] + current[2] + current[3], 1.0)
        current = [c * ratio for c in current]
        by_kind = by_kind * ratio
    row = lax.broadcasted_iota(jnp.int32, (reps, 8, 128), 1)
    ages_full = jnp.broadcast_to(by_age[3], (reps, 8, 128))
    for a in range(AGES - 1):
        ages_full = jnp.where(row == a, by_age[a], ages_full)
    return jnp.concatenate([ages_full, by_kind], axis=1).reshape(reps * 16, 128)


def finish_kernel(
    owners, parts, tables, county, goals, raked, spread,
    hot, partial_a, partial_b, inbox_a, inbox_b, factors_a, factors_b, picked, moments, arrived, shares,
    sum_send, sum_recv, factor_send, factor_recv, part_send, part_recv, share_send, share_recv,
):
    me = lax.axis_index("rows")
    mine = lax.axis_index("rep")
    width, groups = tables.shape
    reps = width // CELLS
    counties = hot.shape[0]
    here = counties // owners
    quarter = groups // parts
    barrier = pltpu.get_barrier_semaphore()
    for d in range(1, owners):
        pl.semaphore_signal(barrier, inc=1, device_id={"rows": lax.rem(me + d, owners)}, device_id_type=MESH)
    for d in range(1, parts):
        pl.semaphore_signal(barrier, inc=1, device_id={"rep": lax.rem(mine + d, parts)}, device_id_type=MESH)

    ids = lax.broadcasted_iota(jnp.int32, (counties, groups), 0)
    is_member = (ids == jnp.broadcast_to(county[...], (counties, groups))).astype(jnp.float32)
    hot[...] = is_member.astype(jnp.bfloat16)
    partial_a[:, CUT * CELLS :] = jnp.broadcast_to(jnp.sum(is_member, axis=1, keepdims=True), (counties, 128))
    contract = (((1,), (1,)), ((), ()))

    def county_sums(low, high):
        upper, lower = pieces(tables[low * CELLS : high * CELLS, :])
        return lax.dot_general(
            hot[...], upper, contract, preferred_element_type=jnp.float32
        ) + lax.dot_general(hot[...], lower, contract, preferred_element_type=jnp.float32)

    def rows_of(owner):
        return pl.ds(pl.multiple_of(owner * here, here), here)

    def send_sums(partial, inbox, half):
        copies = []
        for d in range(1, owners):
            target = lax.rem(me + d, owners)
            copy = pltpu.make_async_remote_copy(
                src_ref=partial.at[rows_of(target)],
                dst_ref=inbox.at[d - 1],
                send_sem=sum_send.at[half, d - 1],
                recv_sem=sum_recv.at[half, d - 1],
                device_id={"rows": target},
                device_id_type=MESH,
            )
            copy.start()
            copies.append(copy)
        return copies

    def receive_sums(partial, inbox, copies):
        total = partial[rows_of(me), :]
        for d in range(1, owners):
            copies[d - 1].wait_recv()
            total = total + inbox[d - 1]
        return jnp.concatenate([total, jnp.zeros((128 - here, total.shape[1]), jnp.float32)], axis=0).T

    def send_factors(found, factors, half):
        room = factors.shape[1]
        if room > found.shape[0]:
            found = jnp.concatenate([found, jnp.zeros((room - found.shape[0], 128), jnp.float32)], axis=0)
        factors[rows_of(me), :] = found.T[:here, :]
        copies = []
        for d in range(1, owners):
            copy = pltpu.make_async_remote_copy(
                src_ref=factors.at[rows_of(me)],
                dst_ref=factors.at[rows_of(me)],
                send_sem=factor_send.at[half, d - 1],
                recv_sem=factor_recv.at[half, d - 1],
                device_id={"rows": lax.rem(me + d, owners)},
                device_id_type=MESH,
            )
            copy.start()
            copies.append(copy)
        return copies

    def pick(factors, copies, low, high):
        for copy in copies:
            copy.wait_recv()
        upper, lower = pieces(factors[...].T)
        found = jnp.dot(upper, hot[...], preferred_element_type=jnp.float32) + jnp.dot(
            lower, hot[...], preferred_element_type=jnp.float32
        )
        picked[low * 16 : high * 16, :] = found[: (high - low) * 16, :]

    partial_a[:, : CUT * CELLS] = county_sums(0, CUT)
    pl.semaphore_wait(barrier, owners - 1 + parts - 1)
    sums_a = send_sums(partial_a, inbox_a, 0)
    partial_b[...] = county_sums(CUT, reps)
    sums_b = send_sums(partial_b, inbox_b, 1)
    columns = receive_sums(partial_a, inbox_a, sums_a)
    member = columns[CUT * CELLS : CUT * CELLS + 8, :]
    gathers_a = send_factors(rake(columns[: CUT * CELLS, :], member, goals[...]), factors_a, 0)
    columns = receive_sums(partial_b, inbox_b, sums_b)
    gathers_b = send_factors(rake(columns, member, goals[...]), factors_b, 1)
    pick(factors_a, gathers_a, 0, CUT)
    pick(factors_b, gathers_b, CUT, reps)
    sums, gathers = sums_a + sums_b, gathers_a + gathers_b

    def work(part):
        for t in range(quarter // 128):
            lanes = pl.ds(pl.multiple_of(part * quarter + t * 128, 128), 128)
            inner = pl.ds(t * 128, 128)
            count = [jnp.zeros((8, 128), jnp.float32) for _ in range(AGES)]
            for r in range(reps):
                by_age = picked[r * 16 : r * 16 + 8, lanes]
                by_kind = picked[r * 16 + 8 : r * 16 + 16, lanes]
                for a in range(AGES):
                    at = r * CELLS + a * 8
                    value = tables[at : at + 8, lanes] * (by_kind * by_age[a : a + 1, :])
                    raked[at : at + 8, lanes] = value
                    count[a] = count[a] + value
            for a in range(AGES):
                mean = count[a] / reps
                within = jnp.zeros((8, 128), jnp.float32)
                for r in range(reps):
                    at = r * CELLS + a * 8
                    within = within + jnp.square(raked[at : at + 8, lanes] - mean)
                moments[part, a * 8 : a * 8 + 8, inner] = mean
                moments[part, CELLS + a * 8 : CELLS + a * 8 + 8, inner] = within

    sends = []
    for d in range(1, parts):
        target = lax.rem(mine + d, parts)
        work(target)
        copy = pltpu.make_async_remote_copy(
            src_ref=moments.at[target],
            dst_ref=arrived.at[d - 1],
            send_sem=part_send.at[d - 1],
            recv_sem=part_recv.at[d - 1],
            device_id={"rep": target},
            device_id_type=MESH,
        )
        copy.start()
        sends.append(copy)
    work(mine)
    own = moments[mine]
    both = [own]
    for d in range(1, parts):
        sends[d - 1].wait_recv()
        both.append(arrived[d - 1])
    centre = both[0][:CELLS]
    for other in both[1:]:
        centre = centre + other[:CELLS]
    centre = centre / parts
    deviation = jnp.zeros((CELLS, quarter), jnp.float32)
    for other in both:
        deviation = deviation + (other[CELLS:] + reps * jnp.square(other[:CELLS] - centre))
    shares[mine] = deviation * (4.0 / (reps * parts))
    answers = []
    for d in range(1, parts):
        target = lax.rem(mine + d, parts)
        copy = pltpu.make_async_remote_copy(
            src_ref=shares.at[mine],
            dst_ref=shares.at[mine],
            send_sem=share_send.at[d - 1],
            recv_sem=share_recv.at[d - 1],
            device_id={"rep": target},
            device_id_type=MESH,
        )
        copy.start()
        answers.append(copy)
    for copy in answers:
        copy.wait_recv()
    for part in range(parts):
        spread[:, part * quarter : (part + 1) * quarter] = shares[part]
    for copy in sums + gathers + sends + answers:
        copy.wait_send()


def local(weights, cell_ids, group_sizes, group_county, age_rate, kind_rate):
    owners, parts = lax.axis_size("rows"), lax.axis_size("rep")
    tables = tabulate(weights, cell_ids, group_sizes)
    width, groups = tables.shape
    here = age_rate.shape[0]
    counties = here * owners
    cut_width = CUT * CELLS
    rest_width = width - cut_width
    goals = jnp.concatenate([age_rate.T, jnp.zeros((8 - AGES, here), jnp.float32), kind_rate.T], axis=0)
    goals = jnp.pad(goals, ((0, 0), (0, 128 - here)))
    quarter = groups // parts
    vmem = pl.BlockSpec(memory_space=pltpu.VMEM)
    dma = pltpu.SemaphoreType.DMA
    raked, spread = pl.pallas_call(
        functools.partial(finish_kernel, owners, parts),
        out_shape=(
            jax.ShapeDtypeStruct((width, groups), jnp.float32),
            jax.ShapeDtypeStruct((CELLS, groups), jnp.float32),
        ),
        in_specs=[vmem] * 3,
        out_specs=(vmem, vmem),
        scratch_shapes=[
            pltpu.VMEM((counties, groups), jnp.bfloat16),
            pltpu.VMEM((counties, cut_width + 128), jnp.float32),
            pltpu.VMEM((counties, rest_width), jnp.float32),
            pltpu.VMEM((owners - 1, here, cut_width + 128), jnp.float32),
            pltpu.VMEM((owners - 1, here, rest_width), jnp.float32),
            pltpu.VMEM((counties, -(-cut_width // 256) * 128), jnp.float32),
            pltpu.VMEM((counties, -(-rest_width // 256) * 128), jnp.float32),
            pltpu.VMEM((width // 2, groups), jnp.float32),
            pltpu.VMEM((parts, 2 * CELLS, quarter), jnp.float32),
            pltpu.VMEM((parts - 1, 2 * CELLS, quarter), jnp.float32),
            pltpu.VMEM((parts, CELLS, quarter), jnp.float32),
            dma((2, owners - 1)),
            dma((2, owners - 1)),
            dma((2, owners - 1)),
            dma((2, owners - 1)),
            dma((parts - 1,)),
            dma((parts - 1,)),
            dma((parts - 1,)),
            dma((parts - 1,)),
        ],
        compiler_params=pltpu.CompilerParams(
            collective_id=0, has_side_effects=True, vmem_limit_bytes=48 * 1024 * 1024
        ),
    )(tables, group_county.reshape(1, groups), goals)
    return raked.T, spread.T


def solution(mesh):
    placed = (
        P("rep", "rows"),
        P("rows"),
        P("rows", None),
        P("rows", None),
        P("rows", None),
        P("rows", None),
    )
    return jax.shard_map(
        local,
        mesh=mesh,
        in_specs=placed,
        out_specs=(P("rows", "rep"), P("rows", None)),
        check_vma=False,
    )
```

time: 77 us -> 62.9 us (0.82)
  Pallas kernels: 67.2 us -> 53.2 us
    pallas_call x1, Pallas kernels: 31.6 us -> 20.5 us  [tabulate(): pl.pallas_call(tabulate_kernel, out_shape=jax.ShapeDtypeStruct((reps * CE...]
    pallas_call x1, Pallas kernels: 35.5 us -> 32.7 us  [local(): pl.pallas_call(functools.partial(finish_kernel, owners, parts), out_shape...]
where the time goes in v3:
time: 62.9 us; the launch traced here: 62.6 us
  Pallas kernels  53.2 us (85%)
  local copies, waits for them, and re-layouts  5.67 us (9%)
  other arithmetic  1.68 us (3%)
  matrix products  1.34 us (2%)
  between operations  0.68 us (1%)
    pallas_call x1, Pallas kernels, local(): pl.pallas_call(functools.partial(finish_kernel, owners, parts), out_shape...  32.7 us
    pallas_call x1, Pallas kernels, tabulate(): pl.pallas_call(tabulate_kernel, out_shape=jax.ShapeDtypeStruct((reps * CE...  20.5 us
    unnamed x8, local copies, waits for them, and re-layouts  5.59 us
    dot_general x1, matrix products, exact_dot(): jnp.dot(left, right, precision=lax.Precision.HIGHEST, preferred_element_t...  1.34 us

profile of v3, /device:TPU:0, one launch (start us, length us, event | category | flops | bytes accessed | tf_op | source)
XLA Modules:
  0.0 62.6 jit_solution(8392408539217948691)
XLA Ops:
  0.6 0.1 pad.7.clone
  0.7 1.3 %fusion = f32[1,1024]{1,0:T(1,128)S(1)} fusion(s32[1,1024]{1,0:T(1,128)} %param.8), kind=kOutput, calls=%fused_computation.1 | convolution fusion | flops 13632512 | bytes 8192 | tf_op jit(solution)/shard_map/dot_general | solution.py:24
  2.1 0.0 copy-start.2
  2.1 0.7 %convert_subtract_fusion = s32[1024]{0:T(1024)S(1)} fusion(s32[1024]{0:T(1024)} %bitcast.18, f32[1024]{0:T(1024)S(1)} %bitcast.16), kind=kLoop, calls=%fused_computation.7 | loop fusion | flops 2048 | bytes 12288 | tf_op jit(solution)/shard_map/sub | solution.py:118
  2.8 0.2 convert_reduce_fusion.first
  3.0 0.8 %pad_maximum_fusion = f32[16,32]{1,0:T(8,128)S(1)} fusion(f32[8,32]{1,0:T(8,128)} %bitcast.19, f32[4,32]{1,0:T(4,128)} %bitcast.20, f32[16]{0:T(128)S(1)} %pad.7.clone), kind=kLoop, calls=%fused_computation.3 | loop fusion | flops 1024 | bytes 3648 | tf_op jit(solution)/shard_map/concatenate | solution.py:340
  3.8 0.0 copy-start
  3.8 1.9 %copy-done = bf16[20,65536]{1,0:T(8,128)(2,1)S(1)} copy-done((bf16[20,65536]{1,0:T(8,128)(2,1)S(1)}, bf16[20,65536]{1,0:T(8,128)(2,1)}, u32[]{:S(2)}) %copy-start) | copy-done | bytes 2621464
  5.7 0.0 copy-start.1
  5.7 0.9 %copy-done.1 = s32[65536]{0:T(1024)S(1)} copy-done((s32[65536]{0:T(1024)S(1)}, s32[65536]{0:T(1024)}, u32[]{:S(2)}) %copy-start.1) | copy-done | bytes 262168
  6.6 20.5 %shard_map.77.tables = f32[640,1024]{1,0:T(8,128)S(1)} custom-call(s32[1152]{0:T(1024)S(1)} %concatenate.6.starts, s32[64]{0:T(128)S(1)} %convert_reduce_fusion.first, bf16[20,65536]{1,0:T(8,128)(2,1)S(1)} %copy-done, s32[512,128]{1,0:T(8,128)S(1)} %bitcast.13), custom_call_target="tpu_custom_call" | custom-call | tf_op jit(solution)/shard_map/pallas_call | solution.py:124
  27.1 0.0 copy-done.2
  27.1 32.7 %shard_map.78 = (f32[640,1024]{1,0:T(8,128)S(1)}, f32[32,1024]{1,0:T(8,128)S(1)}) custom-call(f32[640,1024]{1,0:T(8,128)S(1)} %shard_map.77.tables, s32[1,1024]{1,0:T(1,128)S(1)} %bitcast.15, f32[16,128]{1,0:T(8,128)S(1)} %pad.5.goals), custom_call_target="tpu_custom_call" | custom-call | tf_op jit(solution)/shard_map/pallas_call | solution.py:345
  59.8 2.1 %copy.9 = f32[1024,640]{1,0:T(8,128)} copy(f32[1024,640]{0,1:T(8,128)S(1)} %bitcast.12) | data formatting | bytes 5242880
  61.9 0.7 %copy.11 = f32[1024,32]{0,1:T(8,128)} copy(f32[1024,32]{0,1:T(8,128)S(1)} %bitcast.14) | data formatting | bytes 262144
  (5 shorter events, 0.0 us)
Async XLA Ops:
  2.1 25.0 %copy-start.2 = (s32[1024,1]{0,1:T(1,128)S(1)}, s32[1024,1]{0,1:T(1,128)}, u32[]{:S(2)}) copy-start(s32[1024,1]{0,1:T(1,128)} %param.9) | copy-start | bytes 12292
  3.8 1.9 %copy-start = (bf16[20,65536]{1,0:T(8,128)(2,1)S(1)}, bf16[20,65536]{1,0:T(8,128)(2,1)}, u32[]{:S(2)}) copy-start(bf16[20,65536]{1,0:T(8,128)(2,1)} %weights.1) | copy-start | bytes 7864324
  5.7 0.9 %copy-start.1 = (s32[65536]{0:T(1024)S(1)}, s32[65536]{0:T(1024)}, u32[]{:S(2)}) copy-start(s32[65536]{0:T(1024)} %param.7) | copy-start | bytes 786436

commit v4 on v3

--- a/solution.py
+++ b/solution.py
@@ -104,7 +104,7 @@
         add_block(i * STEP, STEP)
         return carry
 
-    lax.fori_loop(0, whole, step, 0)
+    lax.fori_loop(0, whole, step, 0, unroll=3)
     if units % STEP:
         add_block(whole * STEP, units % STEP)
 

time: 62.9 us -> 60.1 us (0.955)
  Pallas kernels: 53.2 us -> 50.5 us
    pallas_call x1, Pallas kernels: 20.5 us -> 17.8 us  [tabulate(): pl.pallas_call(tabulate_kernel, out_shape=jax.ShapeDtypeStruct((reps * CE...]
where the time goes in v4:
time: 60.1 us; the launch traced here: 59.9 us
  Pallas kernels  50.5 us (84%)
  local copies, waits for them, and re-layouts  5.67 us (9%)
  other arithmetic  1.68 us (3%)
  matrix products  1.34 us (2%)
  between operations  0.68 us (1%)
    pallas_call x1, Pallas kernels, local(): pl.pallas_call(functools.partial(finish_kernel, owners, parts), out_shape...  32.7 us
    pallas_call x1, Pallas kernels, tabulate(): pl.pallas_call(tabulate_kernel, out_shape=jax.ShapeDtypeStruct((reps * CE...  17.8 us
    unnamed x8, local copies, waits for them, and re-layouts  5.59 us
    dot_general x1, matrix products, exact_dot(): jnp.dot(left, right, precision=lax.Precision.HIGHEST, preferred_element_t...  1.34 us

profile of v4, /device:TPU:0, one launch (start us, length us, event | category | flops | bytes accessed | tf_op | source)
XLA Modules:
  0.0 59.9 jit_solution(9135985900532762143)
XLA Ops:
  0.6 0.1 pad.7.clone
  0.7 1.3 %fusion = f32[1,1024]{1,0:T(1,128)S(1)} fusion(s32[1,1024]{1,0:T(1,128)} %param.8), kind=kOutput, calls=%fused_computation.1 | convolution fusion | flops 13632512 | bytes 8192 | tf_op jit(solution)/shard_map/dot_general | solution.py:24
  2.1 0.0 copy-start.2
  2.1 0.7 %convert_subtract_fusion = s32[1024]{0:T(1024)S(1)} fusion(s32[1024]{0:T(1024)} %bitcast.18, f32[1024]{0:T(1024)S(1)} %bitcast.16), kind=kLoop, calls=%fused_computation.7 | loop fusion | flops 2048 | bytes 12288 | tf_op jit(solution)/shard_map/sub | solution.py:118
  2.8 0.2 convert_reduce_fusion.first
  3.0 0.8 %pad_maximum_fusion = f32[16,32]{1,0:T(8,128)S(1)} fusion(f32[8,32]{1,0:T(8,128)} %bitcast.19, f32[4,32]{1,0:T(4,128)} %bitcast.20, f32[16]{0:T(128)S(1)} %pad.7.clone), kind=kLoop, calls=%fused_computation.3 | loop fusion | flops 1024 | bytes 3648 | tf_op jit(solution)/shard_map/concatenate | solution.py:340
  3.8 0.0 copy-start
  3.8 1.9 %copy-done = bf16[20,65536]{1,0:T(8,128)(2,1)S(1)} copy-done((bf16[20,65536]{1,0:T(8,128)(2,1)S(1)}, bf16[20,65536]{1,0:T(8,128)(2,1)}, u32[]{:S(2)}) %copy-start) | copy-done | bytes 2621464
  5.7 0.0 copy-start.1
  5.7 0.9 %copy-done.1 = s32[65536]{0:T(1024)S(1)} copy-done((s32[65536]{0:T(1024)S(1)}, s32[65536]{0:T(1024)}, u32[]{:S(2)}) %copy-start.1) | copy-done | bytes 262168
  6.6 17.8 %shard_map.77.tables = f32[640,1024]{1,0:T(8,128)S(1)} custom-call(s32[1152]{0:T(1024)S(1)} %concatenate.6.starts, s32[64]{0:T(128)S(1)} %convert_reduce_fusion.first, bf16[20,65536]{1,0:T(8,128)(2,1)S(1)} %copy-done, s32[512,128]{1,0:T(8,128)S(1)} %bitcast.13), custom_call_target="tpu_custom_call" | custom-call | tf_op jit(solution)/shard_map/pallas_call | solution.py:124
  24.4 0.0 copy-done.2
  24.4 32.7 %shard_map.78 = (f32[640,1024]{1,0:T(8,128)S(1)}, f32[32,1024]{1,0:T(8,128)S(1)}) custom-call(f32[640,1024]{1,0:T(8,128)S(1)} %shard_map.77.tables, s32[1,1024]{1,0:T(1,128)S(1)} %bitcast.15, f32[16,128]{1,0:T(8,128)S(1)} %pad.5.goals), custom_call_target="tpu_custom_call" | custom-call | tf_op jit(solution)/shard_map/pallas_call | solution.py:345
  57.1 2.1 %copy.9 = f32[1024,640]{1,0:T(8,128)} copy(f32[1024,640]{0,1:T(8,128)S(1)} %bitcast.12) | data formatting | bytes 5242880
  59.2 0.7 %copy.11 = f32[1024,32]{0,1:T(8,128)} copy(f32[1024,32]{0,1:T(8,128)S(1)} %bitcast.14) | data formatting | bytes 262144
  (5 shorter events, 0.0 us)
Async XLA Ops:
  2.1 22.3 %copy-start.2 = (s32[1024,1]{0,1:T(1,128)S(1)}, s32[1024,1]{0,1:T(1,128)}, u32[]{:S(2)}) copy-start(s32[1024,1]{0,1:T(1,128)} %param.9) | copy-start | bytes 12292
  3.8 1.9 %copy-start = (bf16[20,65536]{1,0:T(8,128)(2,1)S(1)}, bf16[20,65536]{1,0:T(8,128)(2,1)}, u32[]{:S(2)}) copy-start(bf16[20,65536]{1,0:T(8,128)(2,1)} %weights.1) | copy-start | bytes 7864324
  5.7 0.9 %copy-start.1 = (s32[65536]{0:T(1024)S(1)}, s32[65536]{0:T(1024)}, u32[]{:S(2)}) copy-start(s32[65536]{0:T(1024)} %param.7) | copy-start | bytes 786436
